TPU v7x, 512 devices: a whole 4x4x16 slice. The times are simulated.
512 devices in a mesh: ctx: 32 (over z, core), exp: 16 (over y, x).
Axes of the slice: x: 4, y: 4, z: 16, core: 2. Of those that a mesh axis runs over, the one named last changes fastest.
Arguments:
- x_in: bfloat16 [4096, 4096], P('ctx', 'exp'), may hold values from -6 to 6
- z_gate: bfloat16 [4096, 4096], P('ctx', 'exp'), may hold values from -6 to 6
- b_proj: bfloat16 [4096, 128], P('ctx'), may hold values from -0.5 to 0.5
- c_proj: bfloat16 [4096, 128], P('ctx'), may hold values from -0.5 to 0.5
- dt_raw: float32 [64, 4096], P('exp', 'ctx'), may hold values from -4 to 4
- a_log: float32 [64], P('exp'), may hold values from -13 to -2.9
- d_skip: float32 [64], P('exp'), may hold values from 0.5 to 1.5
- out_proj: bfloat16 [4096, 2048], P('exp'), may hold values from -0.09375 to 0.09375
- residual: bfloat16 [4096, 2048], P('ctx'), may hold values from -80 to 80
- norm_gain: float32 [2048], replicated, may hold values from 0.5 to 1.5
- router: bfloat16 [2048, 16], replicated, may hold values from -0.125 to 0.125
- w_gate: bfloat16 [16, 2048, 7168], P(None, 'ctx', 'exp'), may hold values from -0.125 to 0.125
- w_up: bfloat16 [16, 2048, 7168], P(None, 'ctx', 'exp'), may hold values from -0.125 to 0.125
- w_down: bfloat16 [16, 2048, 7168], P(None, 'ctx', 'exp'), may hold values from -0.0625 to 0.0625
- block_experts: int32 [32, 2], replicated, may hold values from 0 to 15, all different within a row
Outputs:
- stream_out: bfloat16 [4096, 2048], P('ctx', 'exp')
- expert_out: bfloat16 [4096, 2048], P('ctx', 'exp')
All inputs are finite; a program needn't handle non-finite values.
Results may differ from a plain program's by a relative error of at most 0.03.
Values may be sent and summed in bfloat16 or wider, within the bound.
A program may use at most 64 MiB of HBM per device.

v0:
```python
import jax
import jax.numpy as jnp
from jax import lax
from jax.sharding import PartitionSpec as P

BLOCK = 128


highest = lax.Precision.HIGHEST
epsilon = 1e-05


def shifted(shard, axis, by):
    size = lax.axis_size(axis)
    pairs = [(i, i + by) for i in range(size) if 0 <= i + by < size]
    return lax.ppermute(shard, axis, pairs)


def block_terms(inputs_f, steps_f, keys_f, queries_f, head_rates):
    length = inputs_f.shape[0]
    log_decay = -head_rates[:, None] * steps_f
    running = jnp.cumsum(log_decay, axis=1)
    spread = running[:, :, None] - running[:, None, :]
    lower_part = jnp.arange(length)[:, None] >= jnp.arange(length)[None, :]
    weights = jnp.where(lower_part[None], jnp.exp(jnp.minimum(spread, 0.0)), 0.0)
    scores = jnp.dot(queries_f, keys_f.T, precision=highest)
    mixing = scores[None] * weights * steps_f[:, None, :]
    inside = jnp.einsum("hls,shp->lhp", mixing, inputs_f, precision=highest)
    carry_weight = jnp.exp(running[:, -1:] - running) * steps_f
    own_state = jnp.einsum("hs,shp,sn->hpn", carry_weight, inputs_f, keys_f, precision=highest)
    return (inside, own_state, jnp.exp(running), jnp.exp(running[:, -1]))


def per_device(
    x_in,
    z_gate,
    b_proj,
    c_proj,
    dt_raw,
    a_log,
    d_skip,
    out_proj,
    residual,
    norm_gain,
    router,
    w_gate,
    w_up,
    w_down,
    block_experts,
):
    slab_rows = x_in.shape[0]
    head_count = dt_raw.shape[0]
    head_size = x_in.shape[1] // head_count
    blocks_here = slab_rows // BLOCK
    head_rates = jnp.exp(a_log)
    steps_f = jax.nn.softplus(dt_raw).reshape(head_count, blocks_here, BLOCK).transpose(1, 0, 2)
    inputs_f = x_in.astype(jnp.float32).reshape(blocks_here, BLOCK, head_count, head_size)
    keys_f = b_proj.astype(jnp.float32).reshape(blocks_here, BLOCK, -1)
    queries_f = c_proj.astype(jnp.float32).reshape(blocks_here, BLOCK, -1)
    inside, own_state, entry_scale, block_decay = jax.vmap(block_terms, in_axes=(0, 0, 0, 0, None))(
        inputs_f, steps_f, keys_f, queries_f, head_rates
    )
    partial_states = []
    slab_keep = jnp.ones((head_count,), jnp.float32)
    slab_state = jnp.zeros(own_state.shape[1:], jnp.float32)
    kept_decay = slab_keep
    partial_states.append(slab_state)
    slab_state = block_decay[0][:, None, None] * slab_state + own_state[0]
    slab_keep = slab_keep * block_decay[0]

    def relay(turn, arriving):
        return shifted(
            (slab_keep[:, None, None] * arriving + slab_state).astype(jnp.bfloat16), "ctx", 1
        ).astype(jnp.float32)

    incoming = lax.fori_loop(0, lax.axis_size("ctx") - 1, relay, jnp.zeros_like(slab_state))
    entering = jnp.stack([kept_decay[:, None, None] * incoming])
    from_before = entry_scale.transpose(0, 2, 1)[..., None] * jnp.einsum(
        "bln,bhpn->blhp", queries_f, entering, precision=highest
    )
    outputs = inside + from_before + d_skip[None, None, :, None] * inputs_f
    gated_rows = (outputs.reshape(slab_rows, -1) * jax.nn.silu(z_gate.astype(jnp.float32))).astype(
        jnp.bfloat16
    )
    group_term = jnp.dot(gated_rows, out_proj, preferred_element_type=jnp.float32).astype(
        jnp.bfloat16
    )
    model_width = residual.shape[1]
    share_cols = model_width // lax.axis_size("exp")
    first_col = lax.axis_index("exp") * share_cols
    mixed_sum = lax.psum(group_term, "exp").astype(jnp.float32)
    stream_full = mixed_sum + residual.astype(jnp.float32)
    mean_square = jnp.mean(stream_full * stream_full, axis=1, keepdims=True)
    normed = (stream_full * lax.rsqrt(mean_square + epsilon) * norm_gain).astype(jnp.bfloat16)
    stream_share = lax.dynamic_slice_in_dim(stream_full, first_col, share_cols, 1)
    expert_count = router.shape[1]
    logits = jnp.dot(normed, router, preferred_element_type=jnp.float32).reshape(
        blocks_here, BLOCK, expert_count
    )
    named_here = lax.dynamic_slice_in_dim(
        block_experts, lax.axis_index("ctx") * blocks_here, blocks_here, 0
    )
    one_hot = (
        named_here[:, :, None] == jnp.arange(expert_count, dtype=jnp.int32)[None, None, :]
    ).astype(jnp.float32)
    chosen = jnp.einsum("bte,bse->bts", logits, one_hot, precision=highest)
    mixing_gates = jax.nn.sigmoid(chosen - chosen[:, :, ::-1])
    flat_named = block_experts.reshape(-1)
    sent_gate = jnp.take(w_gate, flat_named, axis=0)
    sent_up = jnp.take(w_up, flat_named, axis=0)
    sent_down = jnp.take(w_down, flat_named, axis=0)
    got_gate, got_up, got_down = (
        lax.all_to_all(sent_gate, "ctx", split_axis=0, concat_axis=1, tiled=True),
        lax.all_to_all(sent_up, "ctx", split_axis=0, concat_axis=1, tiled=True),
        lax.all_to_all(sent_down, "ctx", split_axis=0, concat_axis=1, tiled=True),
    )
    full_gate = got_gate.reshape(blocks_here, 2, model_width, -1)
    full_up = got_up.reshape(blocks_here, 2, model_width, -1)
    full_down = got_down.reshape(blocks_here, 2, model_width, -1)
    rows_in = normed.reshape(blocks_here, BLOCK, model_width)
    gate_part = jnp.einsum("btd,bkdf->bktf", rows_in, full_gate, preferred_element_type=jnp.float32)
    up_part = jnp.einsum("btd,bkdf->bktf", rows_in, full_up, preferred_element_type=jnp.float32)
    hidden = (jax.nn.silu(gate_part) * up_part).astype(jnp.bfloat16)
    down_part = jnp.einsum("bktf,bkdf->bktd", hidden, full_down, preferred_element_type=jnp.float32)
    weighted = jnp.sum(mixing_gates.transpose(0, 2, 1)[..., None] * down_part, axis=1).reshape(
        slab_rows, model_width
    )
    expert_share = lax.psum_scatter(
        weighted.astype(jnp.bfloat16), "exp", scatter_dimension=1, tiled=True
    )
    return (stream_share.astype(jnp.bfloat16), expert_share)


def solution(mesh):
    placed = (
        P("ctx", "exp"),
        P("ctx", "exp"),
        P("ctx", None),
        P("ctx", None),
        P("exp", "ctx"),
        P("exp"),
        P("exp"),
        P("exp", None),
        P("ctx", None),
        P(),
        P(),
        P(None, "ctx", "exp"),
        P(None, "ctx", "exp"),
        P(None, "ctx", "exp"),
        P(),
    )
    return jax.shard_map(
        per_device,
        mesh=mesh,
        in_specs=placed,
        out_specs=(P("ctx", "exp"), P("ctx", "exp")),
        check_vma=False,
    )
```

profile of v0, /device:TPU:6, one launch (start us, length us, event | category | flops | bytes accessed | tf_op | source)
XLA Modules:
  0.0 1058.6 jit_solution(5072608627155439137)
XLA Ops:
  16.7 7.0 broadcast_select_fusion.2
  23.7 206.2 %all_to_all.45 = bf16[64,64,448]{2,1,0:T(8,128)(2,1)} all-to-all(bf16[64,64,448]{2,1,0:T(8,128)(2,1)S(1)} %get-tuple-element.53), channel_id=1, replica_groups=mesh['ctx'=32,'exp'=16] {'ctx'}, dimensions={0} | all-to-all | bytes 7340032 | tf_op jit(solution)/shard_map/all_to_all | solution.py:113
  229.9 195.0 %all_to_all.46 = bf16[64,64,448]{2,1,0:T(8,128)(2,1)} all-to-all(bf16[64,64,448]{2,1,0:T(8,128)(2,1)S(1)} %get-tuple-element.54), channel_id=1, replica_groups=mesh['ctx'=32,'exp'=16] {'ctx'}, dimensions={0} | all-to-all | bytes 7340032 | tf_op jit(solution)/shard_map/all_to_all | solution.py:114
  425.0 5.0 all-to-all-start.2
  431.3 364.5 %while.11 = (s32[]{:T(128)}, f32[4,64,128]{2,1,0:T(8,128)S(1)}, f32[1,4]{1,0:T(1,128)S(1)}, f32[4,64,128]{2,1,0:T(8,128)S(1)}, s32[]{:T(128)}, /*index=5*/s32[]{:T(128)}) while((s32[]{:T(128)}, f32[4,64,128]{2,1,0:T(8,128)S(1)}, f32[1,4]{1,0:T(1,128)S(1)}, f32[4,64,128]{2,1,0:T(8,128)S(1)}, s32[]{:T(128)}, ...), condition=%wide.region_2.3_spmd.clone, body=%wide.region_1.2_spmd.clone.sunk | while | flops 163843 | bytes 786567 | solution.py:76
  434.4 171.0 %collective-permute-start = (bf16[4,64,128]{2,1,0:T(8,128)(2,1)S(1)}, bf16[4,64,128]{2,1,0:T(8,128)(2,1)S(1)}, u32[]{:S(2)}, u32[]{:S(2)}) collective-permute-start(bf16[4,64,128]{2,1,0:T(8,128)(2,1)S(1)} %fusion.64), channel_id=1, source_target_pairs={{0,16},{16,32},{32,48},{48,64},{64,80},{80,96},{96,112},{112,128},... | collective-permute-start | bytes 196616 | tf_op jit(solution)/shard_map/while/body/eval_jaxpr/ppermute | solution.py:16
  606.4 10.2 collective-permute-start
  617.7 4.8 collective-permute-start
  623.5 4.7 collective-permute-start
  629.2 4.7 collective-permute-start
  634.9 4.7 collective-permute-start
  640.6 4.7 collective-permute-start
  657.8 4.7 collective-permute-start
  686.3 4.9 collective-permute-start
  692.2 5.9 collective-permute-start
  699.1 5.9 collective-permute-start
  706.0 5.9 collective-permute-start
  712.9 5.9 collective-permute-start
  719.8 5.9 collective-permute-start
  726.7 5.9 collective-permute-start
  733.7 5.9 collective-permute-start
  740.6 5.9 collective-permute-start
  747.5 5.9 collective-permute-start
  754.4 5.9 collective-permute-start
  761.3 5.9 collective-permute-start
  768.2 5.9 collective-permute-start
  775.2 5.9 collective-permute-start
  782.1 5.9 collective-permute-start
  789.0 5.9 collective-permute-start
  798.2 140.1 %all-reduce.2.cloned.1.call-done = bf16[128,2048]{1,0:T(8,128)(2,1)} async-done(((bf16[128,2048]{1,0:T(8,128)(2,1)}), bf16[128,2048]{1,0:T(8,128)(2,1)}) %all-reduce.2.cloned.1.call-update) | async-done | bytes 524304 | tf_op jit(solution)/shard_map/psum | solution.py:91
  954.1 7.9 fusion.2
  963.8 86.5 %reduce-scatter.4.cloned.1.call-done = bf16[128,128]{1,0:T(8,128)(2,1)} async-done(((bf16[2048,128]{1,0:T(8,128)(2,1)}), bf16[128,128]{1,0:T(8,128)(2,1)}) %reduce-scatter.4.cloned.1.call-update) | async-done | bytes 32784
  (180 shorter events, 92.5 us)
Async XLA Ops:
  425.0 524.5 %all-to-all-start.2 = ((bf16[64,64,448]{2,1,0:T(8,128)(2,1)}), bf16[64,64,448]{2,1,0:T(8,128)(2,1)}, u32[]{:S(2)}, u32[]{:S(2)}) async-start(bf16[64,64,448]{2,1,0:T(8,128)(2,1)} %get-tuple-element.55), calls=%async_computation.2 | async-start | bytes 8388608 | tf_op jit(solution)/shard_map/all_to_all | solution.py:115
  430.0 508.4 %all-reduce.2.cloned.1.call-start = ((), (), s32[]{:S(2)}) async-start(), calls=%async_computation.4 | async-start | bytes 1048576 | tf_op jit(solution)/shard_map/psum | solution.py:91
  434.4 171.9 %collective-permute-start = (bf16[4,64,128]{2,1,0:T(8,128)(2,1)S(1)}, bf16[4,64,128]{2,1,0:T(8,128)(2,1)S(1)}, u32[]{:S(2)}, u32[]{:S(2)}) collective-permute-start(bf16[4,64,128]{2,1,0:T(8,128)(2,1)S(1)} %fusion.64), channel_id=1, source_target_pairs={{0,16},{16,32},{32,48},{48,64},{64,80},{80,96},{96,112},{112,128},... | collective-permute-start | bytes 196616 | tf_op jit(solution)/shard_map/while/body/eval_jaxpr/ppermute | solution.py:16
  606.4 11.1 %collective-permute-start = (bf16[4,64,128]{2,1,0:T(8,128)(2,1)S(1)}, bf16[4,64,128]{2,1,0:T(8,128)(2,1)S(1)}, u32[]{:S(2)}, u32[]{:S(2)}) collective-permute-start(bf16[4,64,128]{2,1,0:T(8,128)(2,1)S(1)} %fusion.64), channel_id=1, source_target_pairs={{0,16},{16,32},{32,48},{48,64},{64,80},{80,96},{96,112},{112,128},... | collective-permute-start | bytes 196616 | tf_op jit(solution)/shard_map/while/body/eval_jaxpr/ppermute | solution.py:16
  617.7 5.7 collective-permute-start
  623.5 5.6 collective-permute-start
  629.2 5.6 collective-permute-start
  634.9 5.6 collective-permute-start
  640.6 5.6 collective-permute-start
  646.3 5.6 collective-permute-start
  652.1 5.6 collective-permute-start
  657.8 5.6 collective-permute-start
  663.5 5.6 collective-permute-start
  669.2 5.6 collective-permute-start
  674.9 5.6 collective-permute-start
  686.3 5.7 collective-permute-start
  692.2 6.8 collective-permute-start
  699.1 6.8 collective-permute-start
  706.0 6.8 collective-permute-start
  712.9 6.8 collective-permute-start
  719.8 6.8 collective-permute-start
  726.7 6.8 collective-permute-start
  733.7 6.8 collective-permute-start
  740.6 6.8 collective-permute-start
  747.5 6.8 collective-permute-start
  754.4 6.8 collective-permute-start
  761.3 6.8 collective-permute-start
  768.2 6.8 collective-permute-start
  775.2 6.8 collective-permute-start
  782.1 6.8 collective-permute-start
  789.0 6.8 collective-permute-start
  798.0 252.3 %reduce-scatter.4.cloned.1.call-start = ((), (), s32[]{:S(2)}) async-start(), calls=%async_computation.5 | async-start | bytes 557056
  (19 other events, 3421.4 us)
Sparse Core Ops, SparseCore 0:
  798.1 140.2 all-reduce.1
  963.1 87.0 reduce-scatter.3
where the time goes:
time: 1060 us
  blocking collectives  401 us (38%)
  starting transfers between devices  338 us (32%)
  waiting for transfers between devices  254 us (24%)
  local copies, waits for them, and re-layouts  24 us (2%)
  between operations  14.4 us (1%)
  other arithmetic  13.2 us (1%)
  matrix products  12.6 us (1%)
    ppermute x31, starting transfers between devices, shifted(): return lax.ppermute(shard, axis, pairs)  333 us
    all_to_all x1, blocking collectives, per_device(): lax.all_to_all(sent_gate, 'ctx', split_axis=0, concat_axis=1, tiled=True)  206 us
    all_to_all x1, blocking collectives, per_device(): lax.all_to_all(sent_up, 'ctx', split_axis=0, concat_axis=1, tiled=True)  195 us
    psum x1, waiting for transfers between devices, per_device(): mixed_sum = lax.psum(group_term, 'exp').astype(jnp.float32)  140 us
    unnamed x3, waiting for transfers between devices  86.5 us
    ppermute x31, waiting for transfers between devices, shifted(): return lax.ppermute(shard, axis, pairs)  27.3 us
  transfers between devices with their start and end apart: 34, of which 33 were waited for; matrix products, arithmetic and copies ran while one was open for 2% of the time, Pallas kernels for 0%

commit v1 on v0

v1 whole, which is shorter than its diff:
```python
import functools

import jax
import jax.numpy as jnp
from jax import lax
from jax.experimental import pallas as pl
from jax.experimental.pallas import tpu as pltpu
from jax.sharding import PartitionSpec as P

MESH = pl.DeviceIdType.MESH
F32 = jnp.float32
BF16 = jnp.bfloat16
T = 128
epsilon = 1e-05


def mm(a, b):
    return jnp.dot(a, b, preferred_element_type=F32)


def nt(a, b):
    return lax.dot_general(a, b, (((1,), (1,)), ((), ())), preferred_element_type=F32)


def split2(v):
    hi = v.astype(BF16)
    return hi, (v - hi.astype(F32)).astype(BF16)


def split3(v):
    hi = v.astype(BF16)
    rest = v - hi.astype(F32)
    mid = rest.astype(BF16)
    return hi, mid, (rest - mid.astype(F32)).astype(BF16)


def silu(v):
    return v / (1.0 + jnp.exp(-v))


def kernel(
    nz,
    nx,
    gs,
    x_ref,
    zg_ref,
    b_ref,
    c_ref,
    dt_ref,
    al_ref,
    dk_ref,
    op_ref,
    res_ref,
    gain_ref,
    rt_ref,
    wgu_in,
    wd_in,
    be_ref,
    so_ref,
    eo_ref,
    dt8,
    wgu,
    wd,
    cmsg,
    crcv,
    gbuf,
    tmsg,
    tbuf,
    ysnd,
    yrcv,
    gt,
    rs,
    usnd,
    urcv,
    xs,
    ssnd,
    srcv,
    rp,
    hb,
    os_,
    ob,
    fsnd,
    frcv,
    wl_sem,
    ws_sem,
    wr_sem,
    cs_sem,
    cr_sem,
    as_sem,
    ar_sem,
    bs_sem,
    br_sem,
    ts_sem,
    tr_sem,
    ss_sem,
    sr_sem,
    us_sem,
    ur_sem,
    gs_sem,
    gr_sem,
    rs_sem,
    rr_sem,
    hs_sem,
    hr_sem,
    os_sem,
    or_sem,
):
    ctx = lax.axis_index("ctx")
    q = lax.axis_index("exp")
    z = lax.div(ctx, 2)
    c = lax.rem(ctx, 2)
    ng = nz // gs
    member = lax.rem(z, gs)
    group = lax.div(z, gs)
    up = 2 * lax.rem(z + 1, nz) + c
    down = 2 * lax.rem(z + nz - 1, nz) + c
    other = 2 * z + (1 - c)
    mirror = (2 * q + c, z)
    hops_up = nz // 2
    hops_down = nz - 1 - hops_up

    def remote(src, dst, send, recv, to):
        return pltpu.make_async_remote_copy(
            src_ref=src,
            dst_ref=dst,
            send_sem=send,
            recv_sem=recv,
            device_id=to,
            device_id_type=MESH,
        )

    barrier = pltpu.get_barrier_semaphore()

    def greet(to):
        pl.semaphore_signal(barrier, inc=1, device_id=to, device_id_type=MESH)

    greet((other, q))
    for o in range(1, gs):
        greet((2 * (group * gs + lax.rem(member + o, gs)) + c, q))
    for o in range(1, ng):
        greet((2 * (lax.rem(group + o, ng) * gs + member) + c, q))

    def greet_plane(o, carry):
        greet((ctx, lax.rem(q + o, nx)))
        return carry

    lax.fori_loop(1, nx, greet_plane, 0)

    @pl.when(member == gs - 1)
    def _():
        greet((up, q))

    @pl.when(member == 0)
    def _():
        greet((down, q))

    @pl.when(q != z)
    def _():
        greet(mirror)

    peers = (
        (gs + ng + nx - 2)
        + (member == gs - 1).astype(jnp.int32)
        + (member == 0).astype(jnp.int32)
        + (q != z).astype(jnp.int32)
    )
    pl.semaphore_wait(barrier, peers)

    mine = pl.ds(pl.multiple_of(c * 64, 64), 64)
    theirs = pl.ds(pl.multiple_of((1 - c) * 64, 64), 64)
    w_local = (
        pltpu.make_async_copy(wgu_in, wgu.at[:, mine, :], wl_sem.at[0]),
        pltpu.make_async_copy(wd_in, wd.at[:, mine, :], wl_sem.at[1]),
    )
    w_sent = (
        remote(wgu_in, wgu.at[:, mine, :], ws_sem.at[0], wr_sem.at[0], (other, q)),
        remote(wd_in, wd.at[:, mine, :], ws_sem.at[1], wr_sem.at[1], (other, q)),
    )
    for copy in (*w_sent, *w_local):
        copy.start()

    lane = lax.broadcasted_iota(jnp.int32, (T, T), 1)
    row = lax.broadcasted_iota(jnp.int32, (T, T), 0)
    left = lane < 64
    upper = row < 64
    row8 = lax.broadcasted_iota(jnp.int32, (8, T), 0)
    dt8[...] = jnp.zeros((8, T), F32)
    dt8[0:4, :] = dt_ref[...]
    steps = jnp.log(1.0 + jnp.exp(dt8[...]))
    rate = jnp.zeros((8, T), F32)
    for h in range(4):
        rate = jnp.where(row8 == h, jnp.exp(jnp.full((8, T), al_ref[h], F32)), rate)
    log_decay = -rate * steps
    before = jnp.where(row <= lane, 1.0, 0.0).astype(BF16)
    ones = jnp.ones((T, T), BF16)
    parts = split3(log_decay)
    running = mm(parts[0], before) + (mm(parts[1], before) + mm(parts[2], before))
    totals = mm(parts[0], ones) + (mm(parts[1], ones) + mm(parts[2], ones))
    carry_w = jnp.exp(totals - running) * steps
    turned = jnp.concatenate([running, carry_w, jnp.zeros((T - 16, T), F32)], axis=0).T
    scores = nt(c_ref[...], b_ref[...])
    inside = []
    states = []
    row16 = lax.broadcasted_iota(jnp.int32, (16, T), 0)

    def log_rows(a0, a1):
        h0, l0 = split2(a0)
        h1, l1 = split2(a1)
        return jnp.where(
            row16 == 0,
            h0.astype(F32),
            jnp.where(
                row16 == 1,
                l0.astype(F32),
                jnp.where(
                    row16 == 2,
                    h1.astype(F32),
                    jnp.where(row16 == 3, l1.astype(F32), 0.0),
                ),
            ),
        ).astype(BF16)

    def unpack(message):
        tail = message[T : T + 16, :].astype(F32)
        return message[0:T, :].astype(F32), tail[0:1] + tail[1:2], tail[2:3] + tail[3:4]

    def spread(a0, a1):
        return jnp.where(upper, jnp.exp(a0), jnp.exp(a1))

    for p in range(2):
        xp = x_ref[:, p * T : (p + 1) * T]
        halves = []
        for h in (2 * p, 2 * p + 1):
            gap = turned[:, h : h + 1] - running[h : h + 1, :]
            weight = jnp.exp(jnp.minimum(gap, 0.0)) * steps[h : h + 1, :]
            hi, lo = split2(jnp.where(row >= lane, scores * weight, 0.0))
            halves.append(mm(hi, xp) + mm(lo, xp))
        inside.append(jnp.where(left, halves[0], halves[1]))
        scale = jnp.where(
            left, turned[:, 8 + 2 * p : 9 + 2 * p], turned[:, 9 + 2 * p : 10 + 2 * p]
        )
        hi, lo = split2((xp.astype(F32) * scale).T)
        states.append(mm(hi, b_ref[...]) + mm(lo, b_ref[...]))

    give = jnp.where(c == 0, states[1], states[0])
    keep = jnp.where(c == 0, states[0], states[1])
    a_pairs = [(totals[2 * p : 2 * p + 1, :], totals[2 * p + 1 : 2 * p + 2, :]) for p in range(2)]
    cmsg[0:T, :] = give.astype(BF16)
    cmsg[T : T + 16, :] = log_rows(
        jnp.where(c == 0, a_pairs[1][0], a_pairs[0][0]),
        jnp.where(c == 0, a_pairs[1][1], a_pairs[0][1]),
    )
    to_core = remote(cmsg, crcv, cs_sem.at[0], cr_sem.at[0], (other, q))
    to_core.start()
    own_a0 = jnp.where(c == 0, a_pairs[0][0], a_pairs[1][0])
    own_a1 = jnp.where(c == 0, a_pairs[0][1], a_pairs[1][1])
    to_core.wait_recv()
    got, got_a0, got_a1 = unpack(crcv)
    first = jnp.where(c == 0, keep, got)
    second = jnp.where(c == 0, got, keep)
    first_a0 = jnp.where(c == 0, own_a0, got_a0)
    first_a1 = jnp.where(c == 0, own_a1, got_a1)
    second_a0 = jnp.where(c == 0, got_a0, own_a0)
    second_a1 = jnp.where(c == 0, got_a1, own_a1)
    gbuf[member, 0:T, :] = (spread(second_a0, second_a1) * first + second).astype(BF16)
    gbuf[member, T : T + 16, :] = log_rows(first_a0 + second_a0, first_a1 + second_a1)

    def to_member(o):
        to = 2 * (group * gs + lax.rem(member + o, gs)) + c
        return remote(gbuf.at[member], gbuf.at[member], as_sem.at[o], ar_sem.at[o], (to, q))

    for o in range(1, gs):
        to_member(o).start()
    for o in range(1, gs):
        to_member(o).wait_recv()
    zero = jnp.zeros((T, T), F32)
    zero_row = jnp.zeros((1, T), F32)
    total, total_a0, total_a1 = zero, zero_row, zero_row
    part, part_a0, part_a1 = zero, zero_row, zero_row
    for m in range(gs):
        s, a0, a1 = unpack(gbuf.at[m])
        decay = spread(a0, a1)
        total, total_a0, total_a1 = decay * total + s, total_a0 + a0, total_a1 + a1
        earlier = m < member
        part = jnp.where(earlier, decay * part + s, part)
        part_a0 = jnp.where(earlier, part_a0 + a0, part_a0)
        part_a1 = jnp.where(earlier, part_a1 + a1, part_a1)
    tmsg[0:T, :] = total.astype(BF16)
    tmsg[T : T + 16, :] = log_rows(total_a0, total_a1)

    def to_group(o):
        to = 2 * (lax.rem(group + o, ng) * gs + member) + c
        return remote(tmsg, tbuf.at[o], bs_sem.at[o], br_sem.at[o], (to, q))

    for o in range(1, ng):

        @pl.when(group + o < ng)
        def _(o=o):
            to_group(o).start()

    reach = zero
    for o in range(ng - 1, 0, -1):

        @pl.when(group >= o)
        def _(o=o):
            to_group(o).wait_recv()

        @pl.when(group < o)
        def _(o=o):
            tbuf[o] = jnp.zeros((T + 16, T), BF16)

        s, a0, a1 = unpack(tbuf.at[o])
        reach = jnp.where(group >= o, spread(a0, a1) * reach + s, zero)
    at_first = spread(part_a0, part_a1) * reach + part
    at_second = spread(first_a0, first_a1) * at_first + first
    ysnd[...] = jnp.where(c == 0, at_second, at_first).astype(BF16)
    back = remote(ysnd, yrcv, cs_sem.at[1], cr_sem.at[1], (other, q))
    back.start()
    own_in = jnp.where(c == 0, at_first, at_second).astype(BF16)
    back.wait_recv()
    got_in = yrcv[...]
    entering = (
        jnp.where(c == 0, own_in.astype(F32), got_in.astype(F32)).astype(BF16),
        jnp.where(c == 0, got_in.astype(F32), own_in.astype(F32)).astype(BF16),
    )
    gated = []
    for p in range(2):
        scale = jnp.where(
            left,
            jnp.exp(turned[:, 2 * p : 2 * p + 1]),
            jnp.exp(turned[:, 2 * p + 1 : 2 * p + 2]),
        )
        skip = jnp.where(
            left,
            jnp.full((T, T), dk_ref[2 * p], F32),
            jnp.full((T, T), dk_ref[2 * p + 1], F32),
        )
        xp = x_ref[:, p * T : (p + 1) * T].astype(F32)
        zp = zg_ref[:, p * T : (p + 1) * T].astype(F32)
        out = inside[p] + scale * nt(c_ref[...], entering[p]) + skip * xp
        gated.append((out * silu(zp)).astype(BF16))

    def tile_of(index):
        return pl.ds(pl.multiple_of(index * T, T), T)

    def project(to):
        cols = tile_of(to)
        return mm(gated[0], op_ref[0:T, cols]) + mm(gated[1], op_ref[T : 2 * T, cols])

    def send_term(o):
        to = lax.rem(q + o, nx)
        return remote(gt.at[o], rs.at[o], ts_sem.at[o], tr_sem.at[o], (ctx, to))

    def project_step(o, carry):
        gt[o] = project(lax.rem(q + o, nx)).astype(BF16)
        send_term(o).start()
        return carry

    lax.fori_loop(1, nx, project_step, 0)
    own_term = project(q).astype(BF16).astype(F32)
    stream = own_term + res_ref[:, tile_of(q)].astype(F32)

    def sum_step(o, acc):
        send_term(o).wait_recv()
        return acc + rs[o].astype(F32)

    stream = lax.fori_loop(1, nx, sum_step, stream)
    so_ref[...] = stream.astype(BF16)
    scaled = (stream * gain_ref[:, tile_of(q)]).astype(BF16)
    usnd[...] = scaled
    to_mirror = remote(usnd, urcv, us_sem.at[0], ur_sem.at[0], mirror)

    @pl.when(q != z)
    def _():
        to_mirror.start()

    logits = mm(scaled, rt_ref[tile_of(q), :])
    expert = lax.broadcasted_iota(jnp.int32, (T, rt_ref.shape[1]), 1)
    chosen = jnp.where(expert == be_ref[ctx, 0], logits, 0.0)
    refused = jnp.where(expert == be_ref[ctx, 1], logits, 0.0)
    difference = jnp.sum(chosen - refused, axis=1, keepdims=True)
    square = jnp.sum(stream * stream, axis=1, keepdims=True)
    columns = jnp.where(lane == 0, square, jnp.where(lane == 1, difference, 0.0))
    ssnd[...] = columns.T[0:8, :]

    def send_stat(o):
        return remote(
            ssnd, srcv.at[o], ss_sem.at[o], sr_sem.at[o], (ctx, lax.rem(q + o, nx))
        )

    def stat_step(o, carry):
        send_stat(o).start()
        return carry

    lax.fori_loop(1, nx, stat_step, 0)

    @pl.when(q != z)
    def _():
        to_mirror.wait_recv()
        xs[q] = urcv[...]

    @pl.when(q == z)
    def _():
        xs[q] = usnd[...]

    def send_rows(o):
        to = lax.rem(q + o, nx)
        return remote(xs.at[q], xs.at[q], gs_sem.at[o], gr_sem.at[o], (ctx, to))

    def rows_step(o, carry):
        send_rows(o).start()
        return carry

    lax.fori_loop(1, nx, rows_step, 0)

    def rows_wait(o, carry):
        send_rows(o).wait_recv()
        return carry

    for copy in w_local:
        copy.wait()
    for i in range(2):
        w_sent[i].wait_recv()
    lax.fori_loop(1, nx, rows_wait, 0)

    def partial(d, k):
        return mm(xs[d], wgu[be_ref[2 * d + c, k]])

    def target(way, s):
        if way == 0:
            return lax.rem(z + hops_up - s + nz, nz)
        return lax.rem(z + nz - hops_down + s, nz)

    def send_sum(way, s, k):
        return remote(
            rp.at[way, s, k],
            rp.at[way, s + 1, k],
            rs_sem.at[way, s, k],
            rr_sem.at[way, s, k],
            ((up, down)[way], q),
        )

    ways = tuple(w for w in range(2) if (hops_up, hops_down)[w])
    for k in range(2):
        for way in ways:
            rp[way, 0, k] = partial(target(way, 0), k).astype(BF16)
            send_sum(way, 0, k).start()

    def sum_hop(way, s, k):
        value = partial(target(way, s), k)
        send_sum(way, s - 1, k).wait_recv()
        rp[way, s, k] = (value + rp[way, s, k].astype(F32)).astype(BF16)
        send_sum(way, s, k).start()

    def hop(s, carry):
        for k in range(2):
            for way in range(2):
                sum_hop(way, s, k)
        return carry

    lax.fori_loop(1, hops_down, hop, 0)
    for s in range(max(hops_down, 1), hops_up):
        for k in range(2):
            sum_hop(0, s, k)

    def stat_sum(o, acc):
        send_stat(o).wait_recv()
        return acc + srcv[o]

    stats = lax.fori_loop(1, nx, stat_sum, ssnd[...])
    inverse = lax.rsqrt(stats[0:1, :] * (1.0 / (nx * T)) + epsilon)
    gate0 = 1.0 / (1.0 + jnp.exp(-stats[1:2, :] * inverse))
    gate1 = 1.0 / (1.0 + jnp.exp(stats[1:2, :] * inverse))
    pick = jnp.where(row == 0, inverse, jnp.where(row == 1, gate0, jnp.where(row == 2, gate1, 0.0)))
    turned2 = pick.T
    norm = turned2[:, 0:1]
    rests = []
    for k in range(2):
        value = partial(z, k)
        for way in ways:
            send_sum(way, (hops_up, hops_down)[way] - 1, k).wait_recv()
            value = value + rp[way, (hops_up, hops_down)[way], k].astype(F32)
        value = value * norm
        mix = turned2[:, 1 + k : 2 + k]
        gate_main = value[:, 0:384]
        up_main = value[:, 384:768]
        both = value[:, 768:896]
        hb[z, :, 384 * k : 384 * (k + 1)] = (silu(gate_main) * up_main * mix).astype(BF16)
        swapped = pltpu.roll(both, 64, 1)
        if k == 0:
            rests.append(silu(both) * swapped * mix)
        else:
            rests.append(silu(swapped) * both * mix)
    hb[z, :, 768:896] = jnp.where(left, rests[0], rests[1]).astype(BF16)

    def send_hidden(way, s, part):
        source = lax.rem(z - s + nz, nz) if way == 0 else lax.rem(z + s, nz)
        half = hb.at[source, pl.ds(part * 64, 64), :]
        return remote(
            half,
            half,
            hs_sem.at[way, s, part],
            hr_sem.at[way, s, part],
            ((up, down)[way], q),
        )

    def arrived(way, s, part):
        source = lax.rem(z - 1 - s + nz, nz) if way == 0 else lax.rem(z + 1 + s, nz)
        half = hb.at[source, pl.ds(part * 64, 64), :]
        return remote(
            half,
            half,
            hs_sem.at[way, s, part],
            hr_sem.at[way, s, part],
            ((up, down)[way], q),
        )

    def send_out(d):
        return remote(os_.at[d], ob.at[q], os_sem.at[d], or_sem.at[q], (ctx, d))

    def finish(d):
        e0 = be_ref[2 * d + c, 0]
        e1 = be_ref[2 * d + c, 1]
        w0 = wd[e0]
        w1 = wd[e1]
        rest = jnp.where(left, w0[:, 384:512].astype(F32), w1[:, 384:512].astype(F32)).astype(BF16)
        value = (
            nt(hb[d, :, 0:384], w0[:, 0:384])
            + nt(hb[d, :, 384:768], w1[:, 0:384])
            + nt(hb[d, :, 768:896], rest)
        )
        os_[d] = value.astype(BF16)

        @pl.when(d != q)
        def _():
            send_out(d).start()

    for part in range(2):
        for way in ways:
            send_hidden(way, 0, part).start()
    finish(z)

    def pass_on(s, carry):
        for part in range(2):
            for way in range(2):
                arrived(way, s, part).wait_recv()
                send_hidden(way, s + 1, part).start()
        finish(lax.rem(z - 1 - s + nz, nz))
        finish(lax.rem(z + 1 + s, nz))
        return carry

    lax.fori_loop(0, hops_down - 1, pass_on, 0)
    for s in range(max(hops_down - 1, 0), hops_up):
        for part in range(2):
            for way in ways:
                if s < (hops_up, hops_down)[way]:
                    arrived(way, s, part).wait_recv()
                if s + 1 < (hops_up, hops_down)[way]:
                    send_hidden(way, s + 1, part).start()
        for way in ways:
            if s < (hops_up, hops_down)[way]:
                finish(lax.rem(z - 1 - s + nz, nz) if way == 0 else lax.rem(z + 1 + s, nz))

    def out_sum(o, acc):
        source = lax.rem(q + o, nx)
        remote(os_.at[q], ob.at[source], os_sem.at[q], or_sem.at[source], (ctx, source)).wait_recv()
        return acc + ob[source].astype(F32)

    result = lax.fori_loop(1, nx, out_sum, os_[q].astype(F32)).astype(BF16)
    fsnd[...] = result
    to_owner = remote(fsnd, frcv, us_sem.at[1], ur_sem.at[1], mirror)

    @pl.when(q != z)
    def _():
        to_owner.start()
        to_owner.wait_recv()
        eo_ref[...] = frcv[...]

    @pl.when(q == z)
    def _():
        eo_ref[...] = fsnd[...]

    for copy in (*w_sent, to_core, back):
        copy.wait_send()
    for o in range(1, gs):
        to_member(o).wait_send()
    for o in range(1, ng):

        @pl.when(group + o < ng)
        def _(o=o):
            to_group(o).wait_send()

    @pl.when(q != z)
    def _():
        to_mirror.wait_send()
        to_owner.wait_send()

    def drain(o, carry):
        send_term(o).wait_send()
        send_stat(o).wait_send()
        send_rows(o).wait_send()
        send_out(lax.rem(q + o, nx)).wait_send()
        return carry

    lax.fori_loop(1, nx, drain, 0)

    def drain_up(s, carry):
        for k in range(2):
            send_sum(0, s, k).wait_send()
            send_hidden(0, s, k).wait_send()
        return carry

    def drain_down(s, carry):
        for k in range(2):
            send_sum(1, s, k).wait_send()
            send_hidden(1, s, k).wait_send()
        return carry

    lax.fori_loop(0, hops_up, drain_up, 0)
    lax.fori_loop(0, hops_down, drain_down, 0)


def per_device(
    nz,
    nx,
    gs,
    x_in,
    z_gate,
    b_proj,
    c_proj,
    dt_raw,
    a_log,
    d_skip,
    out_proj,
    residual,
    norm_gain,
    router,
    w_gate,
    w_up,
    w_down,
    block_experts,
):
    experts = w_gate.shape[0]
    wide = 896
    wgu = jnp.concatenate(
        [w_gate[..., :384], w_up[..., :384], w_gate[..., 384:], w_up[..., 384:]], axis=-1
    )
    wd = jnp.concatenate([w_down, w_down[..., 384:]], axis=-1)
    vmem = pl.BlockSpec(memory_space=pltpu.VMEM)
    smem = pl.BlockSpec(memory_space=pltpu.SMEM)
    hbm = pl.BlockSpec(memory_space=pl.ANY)
    dma = pltpu.SemaphoreType.DMA
    hops = nz // 2
    tile = jax.ShapeDtypeStruct((T, T), BF16)
    return pl.pallas_call(
        functools.partial(kernel, nz, nx, gs),
        out_shape=(tile, tile),
        in_specs=[
            vmem,
            vmem,
            vmem,
            vmem,
            vmem,
            smem,
            smem,
            vmem,
            vmem,
            vmem,
            vmem,
            hbm,
            hbm,
            smem,
        ],
        out_specs=(vmem, vmem),
        scratch_shapes=[
            pltpu.VMEM((8, T), F32),
            pltpu.VMEM((experts, T, wide), BF16),
            pltpu.VMEM((experts, T, 512), BF16),
            pltpu.VMEM((T + 16, T), BF16),
            pltpu.VMEM((T + 16, T), BF16),
            pltpu.VMEM((gs, T + 16, T), BF16),
            pltpu.VMEM((T + 16, T), BF16),
            pltpu.VMEM((nz // gs, T + 16, T), BF16),
            pltpu.VMEM((T, T), BF16),
            pltpu.VMEM((T, T), BF16),
            pltpu.VMEM((nx, T, T), BF16),
            pltpu.VMEM((nx, T, T), BF16),
            pltpu.VMEM((T, T), BF16),
            pltpu.VMEM((T, T), BF16),
            pltpu.VMEM((nx, T, T), BF16),
            pltpu.VMEM((8, T), F32),
            pltpu.VMEM((nx, 8, T), F32),
            pltpu.VMEM((2, hops + 1, 2, T, wide), BF16),
            pltpu.VMEM((nz, T, wide), BF16),
            pltpu.VMEM((nx, T, T), BF16),
            pltpu.VMEM((nx, T, T), BF16),
            pltpu.VMEM((T, T), BF16),
            pltpu.VMEM((T, T), BF16),
            dma((2,)),
            dma((2,)),
            dma((2,)),
            dma((2,)),
            dma((2,)),
            dma((gs,)),
            dma((gs,)),
            dma((nz // gs,)),
            dma((nz // gs,)),
            dma((nx,)),
            dma((nx,)),
            dma((nx,)),
            dma((nx,)),
            dma((2,)),
            dma((2,)),
            dma((nx,)),
            dma((nx,)),
            dma((2, hops, 2)),
            dma((2, hops, 2)),
            dma((2, hops, 2)),
            dma((2, hops, 2)),
            dma((nx,)),
            dma((nx,)),
        ],
        compiler_params=pltpu.CompilerParams(
            collective_id=0, has_side_effects=True, vmem_limit_bytes=48 * 2**20
        ),
    )(
        x_in,
        z_gate,
        b_proj,
        c_proj,
        dt_raw,
        a_log,
        d_skip,
        out_proj,
        residual,
        norm_gain.reshape(1, -1),
        router,
        wgu,
        wd,
        block_experts,
    )


def solution(mesh):
    nz = mesh.shape["ctx"] // 2
    nx = mesh.shape["exp"]
    gs = 4 if nz >= 16 else 2
    placed = (
        P("ctx", "exp"),
        P("ctx", "exp"),
        P("ctx", None),
        P("ctx", None),
        P("exp", "ctx"),
        P("exp"),
        P("exp"),
        P("exp", None),
        P("ctx", None),
        P(),
        P(),
        P(None, "ctx", "exp"),
        P(None, "ctx", "exp"),
        P(None, "ctx", "exp"),
        P(),
    )
    return jax.shard_map(
        functools.partial(per_device, nz, nx, gs),
        mesh=mesh,
        in_specs=placed,
        out_specs=(P("ctx", "exp"), P("ctx", "exp")),
        check_vma=False,
    )
```

time: 1060 us -> 218 us (0.21)
  the two profiles are of different devices: /device:TPU:6 before, /device:TPU:16 now
where the time goes in v1:
time: 218 us; the launch traced here: 217 us
  Pallas kernels  204 us (94%)
  local copies, waits for them, and re-layouts  12 us (6%)
    pallas_call x1, Pallas kernels, per_device(): pl.pallas_call(functools.partial(kernel, nz, nx, gs), out_shape=(tile, ti...  204 us
    unnamed x26, local copies, waits for them, and re-layouts  10.5 us

profile of v1, /device:TPU:16, one launch (start us, length us, event | category | flops | bytes accessed | tf_op | source)
XLA Modules:
  0.0 217.3 jit_solution(14085297750333048163)
XLA Ops:
  0.6 0.0 slice-start
  0.6 0.0 slice-start.1
  0.7 0.0 slice-start.2
  0.7 0.0 slice-start.3
  0.7 1.1 slice-done
  1.8 0.1 slice-done.1
  1.8 0.3 slice-done.2
  2.1 0.0 slice-done.3
  2.1 0.0 copy-start.10
  2.1 0.0 slice-start.4
  2.1 0.3 pad_maximum_fusion.wgu_in
  2.5 0.0 copy-start.2
  2.5 0.0 copy-start.3
  2.5 0.9 copy-done.10
  3.4 0.1 slice-done.4
  3.4 0.2 pad_maximum_fusion.1.wd_in
  3.6 1.1 copy.17.rt_ref
  4.8 0.8 copy.18.be_ref
  5.5 0.0 copy-done.2
  5.5 0.0 copy-done.3
  5.5 0.0 copy-start
  5.5 1.2 copy-done
  6.8 1.0 copy-done.1
  7.8 0.8 copy-done.4
  8.6 0.8 copy-done.5
  9.3 0.7 copy-done.6
  10.0 0.7 copy-done.7
  10.7 0.7 copy-done.8
  11.4 0.7 copy-done.9
  12.0 204.0 %shard_map.158 = (bf16[128,128]{1,0:T(8,128)(2,1)S(1)}, bf16[128,128]{1,0:T(8,128)(2,1)S(1)}) custom-call(bf16[128,256]{1,0:T(8,128)(2,1)S(1)} %copy-done.2, bf16[128,256]{1,0:T(8,128)(2,1)S(1)} %copy-done.3, bf16[128,128]{1,0:T(8,128)(2,1)S(1)} %copy-done.4, bf16[128,128]{1,0:T(8,128)(2,1)S(1)} %copy-done.5, f32[4,128]{1,0:T(4,128)S(1)} %copy-done.7, ...), custom_call_target="tpu_custom_call" | custom-call | tf_op jit(solution)/shard_map/pallas_call | solution.py:655
  216.0 0.6 copy.21
  216.7 0.6 copy.22
  (7 shorter events, 0.0 us)
Async XLA Ops:
  0.6 1.1 slice-start
  0.6 1.2 slice-start.1
  0.7 1.4 slice-start.2
  0.7 1.5 slice-start.3
  2.1 1.2 copy-start.10
  2.1 1.3 slice-start.4
  2.5 3.1 %copy-start.2 = (bf16[128,256]{1,0:T(8,128)(2,1)S(1)}, bf16[128,256]{1,0:T(8,128)(2,1)}, u32[]{:S(2)}) copy-start(bf16[128,256]{1,0:T(8,128)(2,1)} %x_ref.1) | copy-start | bytes 196612
  2.5 3.0 %copy-start.3 = (bf16[128,256]{1,0:T(8,128)(2,1)S(1)}, bf16[128,256]{1,0:T(8,128)(2,1)}, u32[]{:S(2)}) copy-start(bf16[128,256]{1,0:T(8,128)(2,1)} %zg_ref.1) | copy-start | bytes 196612
  5.5 1.2 copy-start
  6.8 1.0 copy-start.1
  7.8 0.8 copy-start.4
  8.6 0.8 copy-start.5
  9.3 0.7 copy-start.6
  10.0 0.7 copy-start.7
  10.7 0.7 copy-start.8
  11.4 0.7 copy-start.9

commit v2 on v1

--- a/solution.py
+++ b/solution.py
@@ -42,23 +42,36 @@
     nz,
     nx,
     gs,
+    x_in,
+    zg_in,
+    b_in,
+    c_in,
+    dt_in,
+    al_ref,
+    dk_ref,
+    op_in,
+    res_in,
+    gain_in,
+    rt_in,
+    wg_in,
+    wu_in,
+    wd_in,
+    be_ref,
+    so_ref,
+    eo_ref,
     x_ref,
     zg_ref,
     b_ref,
     c_ref,
     dt_ref,
-    al_ref,
-    dk_ref,
     op_ref,
     res_ref,
     gain_ref,
     rt_ref,
-    wgu_in,
-    wd_in,
-    be_ref,
-    so_ref,
-    eo_ref,
     dt8,
+    wg_stage,
+    wu_stage,
+    wd_stage,
     wgu,
     wd,
     cmsg,
@@ -76,11 +89,16 @@
     ssnd,
     srcv,
     rp,
-    hb,
+    hb0,
+    hb1,
     os_,
     ob,
     fsnd,
     frcv,
+    osnd,
+    orcv,
+    flast,
+    in_sem,
     wl_sem,
     ws_sem,
     wr_sem,
@@ -96,6 +114,8 @@
     sr_sem,
     us_sem,
     ur_sem,
+    ps_sem,
+    pr_sem,
     gs_sem,
     gr_sem,
     rs_sem,
@@ -115,7 +135,9 @@
     up = 2 * lax.rem(z + 1, nz) + c
     down = 2 * lax.rem(z + nz - 1, nz) + c
     other = 2 * z + (1 - c)
-    mirror = (2 * q + c, z)
+    share = lax.rem(q - z + nx, nx)
+    opposite = (2 * share + c, q)
+    home = (ctx, share)
     hops_up = nz // 2
     hops_down = nz - 1 - hops_up
 
@@ -129,6 +151,28 @@
             device_id_type=MESH,
         )
 
+    def tile_of(index):
+        return pl.ds(pl.multiple_of(index * T, T), T)
+
+    inputs = tuple(
+        pltpu.make_async_copy(src, dst, in_sem.at[i])
+        for i, (src, dst) in enumerate(
+            (
+                (dt_in, dt_ref),
+                (b_in, b_ref),
+                (c_in, c_ref),
+                (x_in, x_ref),
+                (zg_in, zg_ref),
+                (op_in, op_ref),
+                (res_in.at[:, tile_of(share)], res_ref),
+                (gain_in.at[:, tile_of(share)], gain_ref),
+                (rt_in.at[:, tile_of(share)], rt_ref),
+            )
+        )
+    )
+    for copy in inputs:
+        copy.start()
+
     barrier = pltpu.get_barrier_semaphore()
 
     def greet(to):
@@ -154,30 +198,45 @@
     def _():
         greet((down, q))
 
-    @pl.when(q != z)
-    def _():
-        greet(mirror)
+    share_up = jnp.logical_and(member == gs - 1, 2 * share + c == up)
+    share_down = jnp.logical_and(member == 0, 2 * share + c == down)
+    near = jnp.logical_or(lax.div(share, gs) == group, lax.rem(share, gs) == member)
+    apart = jnp.logical_not(jnp.logical_or(near, jnp.logical_or(share_up, share_down)))
+
+    @pl.when(apart)
+    def _():
+        greet(opposite)
 
     peers = (
         (gs + ng + nx - 2)
         + (member == gs - 1).astype(jnp.int32)
         + (member == 0).astype(jnp.int32)
-        + (q != z).astype(jnp.int32)
+        + apart.astype(jnp.int32)
     )
-    pl.semaphore_wait(barrier, peers)
 
     mine = pl.ds(pl.multiple_of(c * 64, 64), 64)
-    theirs = pl.ds(pl.multiple_of((1 - c) * 64, 64), 64)
-    w_local = (
-        pltpu.make_async_copy(wgu_in, wgu.at[:, mine, :], wl_sem.at[0]),
-        pltpu.make_async_copy(wd_in, wd.at[:, mine, :], wl_sem.at[1]),
+    w_local = tuple(
+        pltpu.make_async_copy(src, dst, wl_sem.at[i])
+        for i, (src, dst) in enumerate(((wg_in, wg_stage), (wu_in, wu_stage), (wd_in, wd_stage)))
     )
-    w_sent = (
-        remote(wgu_in, wgu.at[:, mine, :], ws_sem.at[0], wr_sem.at[0], (other, q)),
-        remote(wd_in, wd.at[:, mine, :], ws_sem.at[1], wr_sem.at[1], (other, q)),
+    w_sent = tuple(
+        remote(w.at[:, mine, :], w.at[:, mine, :], ws_sem.at[i], wr_sem.at[i], (other, q))
+        for i, w in enumerate((wgu, wd))
     )
-    for copy in (*w_sent, *w_local):
+
+    def pack(e, carry):
+        gate, rise, fall = wg_stage[e], wu_stage[e], wd_stage[e]
+        wgu[e, mine, 0:384] = gate[:, 0:384]
+        wgu[e, mine, 384:768] = rise[:, 0:384]
+        wgu[e, mine, 768:896] = jnp.concatenate([gate[:, 384:448], rise[:, 384:448]], axis=1)
+        wd[e, mine, 0:384] = fall[:, 0:384]
+        wd[e, mine, 384:512] = jnp.concatenate([fall[:, 384:448], fall[:, 384:448]], axis=1)
+        return carry
+
+    for copy in w_local:
         copy.start()
+    for copy in inputs[0:4]:
+        copy.wait()
 
     lane = lax.broadcasted_iota(jnp.int32, (T, T), 1)
     row = lax.broadcasted_iota(jnp.int32, (T, T), 0)
@@ -242,6 +301,8 @@
         hi, lo = split2((xp.astype(F32) * scale).T)
         states.append(mm(hi, b_ref[...]) + mm(lo, b_ref[...]))
 
+    pl.semaphore_wait(barrier, peers)
+
     give = jnp.where(c == 0, states[1], states[0])
     keep = jnp.where(c == 0, states[0], states[1])
     a_pairs = [(totals[2 * p : 2 * p + 1, :], totals[2 * p + 1 : 2 * p + 2, :]) for p in range(2)]
@@ -271,6 +332,9 @@
 
     for o in range(1, gs):
         to_member(o).start()
+    for copy in w_local:
+        copy.wait()
+    lax.fori_loop(0, wg_in.shape[0], pack, 0)
     for o in range(1, gs):
         to_member(o).wait_recv()
     zero = jnp.zeros((T, T), F32)
@@ -316,6 +380,8 @@
     ysnd[...] = jnp.where(c == 0, at_second, at_first).astype(BF16)
     back = remote(ysnd, yrcv, cs_sem.at[1], cr_sem.at[1], (other, q))
     back.start()
+    for copy in w_sent:
+        copy.start()
     own_in = jnp.where(c == 0, at_first, at_second).astype(BF16)
     back.wait_recv()
     got_in = yrcv[...]
@@ -323,6 +389,8 @@
         jnp.where(c == 0, own_in.astype(F32), got_in.astype(F32)).astype(BF16),
         jnp.where(c == 0, got_in.astype(F32), own_in.astype(F32)).astype(BF16),
     )
+    for copy in inputs[4:]:
+        copy.wait()
     gated = []
     for p in range(2):
         scale = jnp.where(
@@ -340,11 +408,8 @@
         out = inside[p] + scale * nt(c_ref[...], entering[p]) + skip * xp
         gated.append((out * silu(zp)).astype(BF16))
 
-    def tile_of(index):
-        return pl.ds(pl.multiple_of(index * T, T), T)
-
     def project(to):
-        cols = tile_of(to)
+        cols = tile_of(lax.rem(to - z + nx, nx))
         return mm(gated[0], op_ref[0:T, cols]) + mm(gated[1], op_ref[T : 2 * T, cols])
 
     def send_term(o):
@@ -358,26 +423,32 @@
 
     lax.fori_loop(1, nx, project_step, 0)
     own_term = project(q).astype(BF16).astype(F32)
-    stream = own_term + res_ref[:, tile_of(q)].astype(F32)
+    stream = own_term + res_ref[...].astype(F32)
 
     def sum_step(o, acc):
         send_term(o).wait_recv()
         return acc + rs[o].astype(F32)
 
     stream = lax.fori_loop(1, nx, sum_step, stream)
-    so_ref[...] = stream.astype(BF16)
-    scaled = (stream * gain_ref[:, tile_of(q)]).astype(BF16)
+    scaled = (stream * gain_ref[...]).astype(BF16)
     usnd[...] = scaled
-    to_mirror = remote(usnd, urcv, us_sem.at[0], ur_sem.at[0], mirror)
-
-    @pl.when(q != z)
-    def _():
-        to_mirror.start()
-
-    logits = mm(scaled, rt_ref[tile_of(q), :])
-    expert = lax.broadcasted_iota(jnp.int32, (T, rt_ref.shape[1]), 1)
-    chosen = jnp.where(expert == be_ref[ctx, 0], logits, 0.0)
-    refused = jnp.where(expert == be_ref[ctx, 1], logits, 0.0)
+    to_opposite = remote(usnd, urcv, us_sem.at[0], ur_sem.at[0], opposite)
+
+    @pl.when(share != z)
+    def _():
+        to_opposite.start()
+
+    osnd[...] = stream.astype(BF16)
+    stream_home = remote(osnd, orcv, ps_sem.at[0], pr_sem.at[0], home)
+
+    @pl.when(share != q)
+    def _():
+        stream_home.start()
+
+    logits = nt(scaled, rt_ref[...])
+    expert = lax.broadcasted_iota(jnp.int32, (T, rt_ref.shape[0]), 1)
+    chosen = jnp.where(expert == be_ref[0, ctx], logits, 0.0)
+    refused = jnp.where(expert == be_ref[1, ctx], logits, 0.0)
     difference = jnp.sum(chosen - refused, axis=1, keepdims=True)
     square = jnp.sum(stream * stream, axis=1, keepdims=True)
     columns = jnp.where(lane == 0, square, jnp.where(lane == 1, difference, 0.0))
@@ -394,18 +465,18 @@
 
     lax.fori_loop(1, nx, stat_step, 0)
 
-    @pl.when(q != z)
-    def _():
-        to_mirror.wait_recv()
-        xs[q] = urcv[...]
-
-    @pl.when(q == z)
-    def _():
-        xs[q] = usnd[...]
+    @pl.when(share != z)
+    def _():
+        to_opposite.wait_recv()
+        xs[share] = urcv[...]
+
+    @pl.when(share == z)
+    def _():
+        xs[share] = usnd[...]
 
     def send_rows(o):
         to = lax.rem(q + o, nx)
-        return remote(xs.at[q], xs.at[q], gs_sem.at[o], gr_sem.at[o], (ctx, to))
+        return remote(xs.at[share], xs.at[share], gs_sem.at[o], gr_sem.at[o], (ctx, to))
 
     def rows_step(o, carry):
         send_rows(o).start()
@@ -413,23 +484,29 @@
 
     lax.fori_loop(1, nx, rows_step, 0)
 
-    def rows_wait(o, carry):
-        send_rows(o).wait_recv()
-        return carry
-
-    for copy in w_local:
-        copy.wait()
-    for i in range(2):
-        w_sent[i].wait_recv()
-    lax.fori_loop(1, nx, rows_wait, 0)
+    def rows_ready(d):
+        source = lax.rem(d + z, nx)
+        o = lax.rem(q - source + nx, nx)
+
+        @pl.when(o != 0)
+        def _():
+            remote(xs.at[d], xs.at[d], gs_sem.at[o], gr_sem.at[o], (ctx, source)).wait_recv()
+
+    for copy in w_sent:
+        copy.wait_recv()
 
     def partial(d, k):
-        return mm(xs[d], wgu[be_ref[2 * d + c, k]])
-
-    def target(way, s):
-        if way == 0:
-            return lax.rem(z + hops_up - s + nz, nz)
-        return lax.rem(z + nz - hops_down + s, nz)
+        return mm(xs[d], wgu[be_ref[k, 2 * d + c]])
+
+    hops = (hops_up, hops_down)
+
+    def goes_up(way, k):
+        return (way == 0) == (k == 0)
+
+    def target(way, s, k):
+        if goes_up(way, k):
+            return lax.rem(z + hops[way] - s + nz, nz)
+        return lax.rem(z + nz - hops[way] + s, nz)
 
     def send_sum(way, s, k):
         return remote(
@@ -437,31 +514,35 @@
             rp.at[way, s + 1, k],
             rs_sem.at[way, s, k],
             rr_sem.at[way, s, k],
-            ((up, down)[way], q),
+            (up if goes_up(way, k) else down, q),
         )
 
-    ways = tuple(w for w in range(2) if (hops_up, hops_down)[w])
+    rows_ready(lax.rem(z + hops_up, nz))
+    for far in (1, nz - 1):
+        rows_ready(lax.rem(z + hops_up + far, nz))
     for k in range(2):
-        for way in ways:
-            rp[way, 0, k] = partial(target(way, 0), k).astype(BF16)
+        for way in range(2):
+            rp[way, 0, k] = partial(target(way, 0, k), k).astype(BF16)
             send_sum(way, 0, k).start()
 
     def sum_hop(way, s, k):
-        value = partial(target(way, s), k)
+        value = partial(target(way, s, k), k)
         send_sum(way, s - 1, k).wait_recv()
         rp[way, s, k] = (value + rp[way, s, k].astype(F32)).astype(BF16)
         send_sum(way, s, k).start()
 
     def hop(s, carry):
+        rows_ready(lax.rem(z + hops_up + 1 + s, nz))
+        rows_ready(lax.rem(z + hops_up - 1 - s + nz, nz))
         for k in range(2):
             for way in range(2):
                 sum_hop(way, s, k)
         return carry
 
     lax.fori_loop(1, hops_down, hop, 0)
-    for s in range(max(hops_down, 1), hops_up):
-        for k in range(2):
-            sum_hop(0, s, k)
+    for k in range(2):
+        sum_hop(0, hops_down, k)
+    rows_ready(z)
 
     def stat_sum(o, acc):
         send_stat(o).wait_recv()
@@ -474,111 +555,124 @@
     pick = jnp.where(row == 0, inverse, jnp.where(row == 1, gate0, jnp.where(row == 2, gate1, 0.0)))
     turned2 = pick.T
     norm = turned2[:, 0:1]
-    rests = []
+    hb = (hb0, hb1)
+
+    def source_of(way, s, k):
+        return lax.rem(z - s + nz, nz) if goes_up(way, k) else lax.rem(z + s, nz)
+
+    def pass_hidden(way, s, k, source):
+        return remote(
+            hb[k].at[source],
+            hb[k].at[source],
+            hs_sem.at[way, s, k],
+            hr_sem.at[way, s, k],
+            (up if goes_up(way, k) else down, q),
+        )
+
+    def send_hidden(way, s, k):
+        return pass_hidden(way, s, k, source_of(way, s, k))
+
+    def arrived(way, s, k):
+        return pass_hidden(way, s, k, source_of(way, s + 1, k))
+
+    rest0 = None
+    own = (partial(z, 0), partial(z, 1))
     for k in range(2):
-        value = partial(z, k)
-        for way in ways:
-            send_sum(way, (hops_up, hops_down)[way] - 1, k).wait_recv()
-            value = value + rp[way, (hops_up, hops_down)[way], k].astype(F32)
+        value = own[k]
+        for way in (1, 0):
+            send_sum(way, hops[way] - 1, k).wait_recv()
+            value = value + rp[way, hops[way], k].astype(F32)
         value = value * norm
         mix = turned2[:, 1 + k : 2 + k]
-        gate_main = value[:, 0:384]
-        up_main = value[:, 384:768]
         both = value[:, 768:896]
-        hb[z, :, 384 * k : 384 * (k + 1)] = (silu(gate_main) * up_main * mix).astype(BF16)
         swapped = pltpu.roll(both, 64, 1)
+        main = (silu(value[:, 0:384]) * value[:, 384:768] * mix).astype(BF16)
         if k == 0:
-            rests.append(silu(both) * swapped * mix)
+            rest0 = silu(both) * swapped * mix
+            hb0[z] = main
         else:
-            rests.append(silu(swapped) * both * mix)
-    hb[z, :, 768:896] = jnp.where(left, rests[0], rests[1]).astype(BF16)
-
-    def send_hidden(way, s, part):
-        source = lax.rem(z - s + nz, nz) if way == 0 else lax.rem(z + s, nz)
-        half = hb.at[source, pl.ds(part * 64, 64), :]
-        return remote(
-            half,
-            half,
-            hs_sem.at[way, s, part],
-            hr_sem.at[way, s, part],
-            ((up, down)[way], q),
-        )
-
-    def arrived(way, s, part):
-        source = lax.rem(z - 1 - s + nz, nz) if way == 0 else lax.rem(z + 1 + s, nz)
-        half = hb.at[source, pl.ds(part * 64, 64), :]
-        return remote(
-            half,
-            half,
-            hs_sem.at[way, s, part],
-            hr_sem.at[way, s, part],
-            ((up, down)[way], q),
-        )
+            hb1[z, :, 0:384] = main
+            hb1[z, :, 384:512] = jnp.where(left, rest0, silu(swapped) * both * mix).astype(BF16)
+        for way in range(2):
+            send_hidden(way, 0, k).start()
 
     def send_out(d):
-        return remote(os_.at[d], ob.at[q], os_sem.at[d], or_sem.at[q], (ctx, d))
+        to = lax.rem(d + z, nx)
+        return remote(os_.at[d], ob.at[q], os_sem.at[d], or_sem.at[q], (ctx, to))
 
     def finish(d):
-        e0 = be_ref[2 * d + c, 0]
-        e1 = be_ref[2 * d + c, 1]
+        e0 = be_ref[0, 2 * d + c]
+        e1 = be_ref[1, 2 * d + c]
         w0 = wd[e0]
         w1 = wd[e1]
         rest = jnp.where(left, w0[:, 384:512].astype(F32), w1[:, 384:512].astype(F32)).astype(BF16)
         value = (
-            nt(hb[d, :, 0:384], w0[:, 0:384])
-            + nt(hb[d, :, 384:768], w1[:, 0:384])
-            + nt(hb[d, :, 768:896], rest)
+            nt(hb0[d], w0[:, 0:384])
+            + nt(hb1[d, :, 0:384], w1[:, 0:384])
+            + nt(hb1[d, :, 384:512], rest)
         )
         os_[d] = value.astype(BF16)
 
-        @pl.when(d != q)
+        @pl.when(d != share)
         def _():
             send_out(d).start()
 
-    for part in range(2):
-        for way in ways:
-            send_hidden(way, 0, part).start()
-    finish(z)
-
-    def pass_on(s, carry):
-        for part in range(2):
-            for way in range(2):
-                arrived(way, s, part).wait_recv()
-                send_hidden(way, s + 1, part).start()
-        finish(lax.rem(z - 1 - s + nz, nz))
-        finish(lax.rem(z + 1 + s, nz))
-        return carry
-
-    lax.fori_loop(0, hops_down - 1, pass_on, 0)
-    for s in range(max(hops_down - 1, 0), hops_up):
-        for part in range(2):
-            for way in ways:
-                if s < (hops_up, hops_down)[way]:
-                    arrived(way, s, part).wait_recv()
-                if s + 1 < (hops_up, hops_down)[way]:
-                    send_hidden(way, s + 1, part).start()
-        for way in ways:
-            if s < (hops_up, hops_down)[way]:
-                finish(lax.rem(z - 1 - s + nz, nz) if way == 0 else lax.rem(z + 1 + s, nz))
+    def pass_on(s, first, both):
+        for k in range(2):
+            arrived(0, s, k).wait_recv()
+            send_hidden(0, s + 1, k).start()
+            arrived(1, s, k).wait_recv()
+            if both:
+                send_hidden(1, s + 1, k).start()
+            if not first:
+                finish(lax.rem(z - s + nz, nz) if k == 0 else lax.rem(z + s, nz))
+            elif k == 0:
+                finish(z)
+
+    def pass_step(s, carry):
+        pass_on(s, False, True)
+        return carry
+
+    pass_on(0, True, hops_down > 1)
+    if hops_down > 1:
+        lax.fori_loop(1, hops_down - 1, pass_step, 0)
+        pass_on(hops_down - 1, False, False)
+    finish(lax.rem(z - hops_down + nz, nz))
+    finish(lax.rem(z + hops_down, nz))
+    for k in range(2):
+        arrived(0, hops_down, k).wait_recv()
+    finish(lax.rem(z + hops_up, nz))
 
     def out_sum(o, acc):
         source = lax.rem(q + o, nx)
-        remote(os_.at[q], ob.at[source], os_sem.at[q], or_sem.at[source], (ctx, source)).wait_recv()
+        remote(os_.at[0], ob.at[source], os_sem.at[0], or_sem.at[source], (ctx, source)).wait_recv()
         return acc + ob[source].astype(F32)
 
-    result = lax.fori_loop(1, nx, out_sum, os_[q].astype(F32)).astype(BF16)
-    fsnd[...] = result
-    to_owner = remote(fsnd, frcv, us_sem.at[1], ur_sem.at[1], mirror)
-
-    @pl.when(q != z)
+    fsnd[...] = lax.fori_loop(1, nx, out_sum, os_[share].astype(F32)).astype(BF16)
+    to_owner = remote(fsnd, frcv, us_sem.at[1], ur_sem.at[1], opposite)
+    owner_home = remote(frcv, flast, ps_sem.at[1], pr_sem.at[1], home)
+
+    @pl.when(share != z)
     def _():
         to_owner.start()
         to_owner.wait_recv()
+
+    @pl.when(share == z)
+    def _():
+        frcv[...] = fsnd[...]
+
+    @pl.when(share != q)
+    def _():
+        owner_home.start()
+        stream_home.wait_recv()
+        so_ref[...] = orcv[...]
+        owner_home.wait_recv()
+        eo_ref[...] = flast[...]
+
+    @pl.when(share == q)
+    def _():
+        so_ref[...] = osnd[...]
         eo_ref[...] = frcv[...]
-
-    @pl.when(q == z)
-    def _():
-        eo_ref[...] = fsnd[...]
 
     for copy in (*w_sent, to_core, back):
         copy.wait_send()
@@ -590,16 +684,21 @@
         def _(o=o):
             to_group(o).wait_send()
 
-    @pl.when(q != z)
-    def _():
-        to_mirror.wait_send()
+    @pl.when(share != z)
+    def _():
+        to_opposite.wait_send()
         to_owner.wait_send()
+
+    @pl.when(share != q)
+    def _():
+        stream_home.wait_send()
+        owner_home.wait_send()
 
     def drain(o, carry):
         send_term(o).wait_send()
         send_stat(o).wait_send()
         send_rows(o).wait_send()
-        send_out(lax.rem(q + o, nx)).wait_send()
+        send_out(lax.rem(share + o, nx)).wait_send()
         return carry
 
     lax.fori_loop(1, nx, drain, 0)
@@ -642,10 +741,6 @@
 ):
     experts = w_gate.shape[0]
     wide = 896
-    wgu = jnp.concatenate(
-        [w_gate[..., :384], w_up[..., :384], w_gate[..., 384:], w_up[..., 384:]], axis=-1
-    )
-    wd = jnp.concatenate([w_down, w_down[..., 384:]], axis=-1)
     vmem = pl.BlockSpec(memory_space=pltpu.VMEM)
     smem = pl.BlockSpec(memory_space=pltpu.SMEM)
     hbm = pl.BlockSpec(memory_space=pl.ANY)
@@ -656,24 +751,37 @@
         functools.partial(kernel, nz, nx, gs),
         out_shape=(tile, tile),
         in_specs=[
-            vmem,
-            vmem,
-            vmem,
-            vmem,
-            vmem,
+            hbm,
+            hbm,
+            hbm,
+            hbm,
+            hbm,
             smem,
             smem,
-            vmem,
-            vmem,
-            vmem,
-            vmem,
+            hbm,
+            hbm,
+            hbm,
+            hbm,
+            hbm,
             hbm,
             hbm,
             smem,
         ],
         out_specs=(vmem, vmem),
         scratch_shapes=[
+            pltpu.VMEM(x_in.shape, BF16),
+            pltpu.VMEM(x_in.shape, BF16),
+            pltpu.VMEM((T, T), BF16),
+            pltpu.VMEM((T, T), BF16),
+            pltpu.VMEM(dt_raw.shape, F32),
+            pltpu.VMEM(out_proj.shape, BF16),
+            pltpu.VMEM((T, T), BF16),
+            pltpu.VMEM((1, T), F32),
+            pltpu.VMEM((experts, T), BF16),
             pltpu.VMEM((8, T), F32),
+            pltpu.VMEM(w_gate.shape, BF16),
+            pltpu.VMEM(w_gate.shape, BF16),
+            pltpu.VMEM(w_gate.shape, BF16),
             pltpu.VMEM((experts, T, wide), BF16),
             pltpu.VMEM((experts, T, 512), BF16),
             pltpu.VMEM((T + 16, T), BF16),
@@ -691,12 +799,17 @@
             pltpu.VMEM((8, T), F32),
             pltpu.VMEM((nx, 8, T), F32),
             pltpu.VMEM((2, hops + 1, 2, T, wide), BF16),
-            pltpu.VMEM((nz, T, wide), BF16),
+            pltpu.VMEM((nz, T, 384), BF16),
+            pltpu.VMEM((nz, T, 512), BF16),
             pltpu.VMEM((nx, T, T), BF16),
             pltpu.VMEM((nx, T, T), BF16),
             pltpu.VMEM((T, T), BF16),
             pltpu.VMEM((T, T), BF16),
-            dma((2,)),
+            pltpu.VMEM((T, T), BF16),
+            pltpu.VMEM((T, T), BF16),
+            pltpu.VMEM((T, T), BF16),
+            dma((9,)),
+            dma((3,)),
             dma((2,)),
             dma((2,)),
             dma((2,)),
@@ -711,6 +824,8 @@
             dma((nx,)),
             dma((2,)),
             dma((2,)),
+            dma((2,)),
+            dma((2,)),
             dma((nx,)),
             dma((nx,)),
             dma((2, hops, 2)),
@@ -721,7 +836,7 @@
             dma((nx,)),
         ],
         compiler_params=pltpu.CompilerParams(
-            collective_id=0, has_side_effects=True, vmem_limit_bytes=48 * 2**20
+            collective_id=0, has_side_effects=True, vmem_limit_bytes=60 * 2**20
         ),
     )(
         x_in,
@@ -734,10 +849,11 @@
         out_proj,
         residual,
         norm_gain.reshape(1, -1),
-        router,
-        wgu,
-        wd,
-        block_experts,
+        router.T,
+        w_gate,
+        w_up,
+        w_down,
+        block_experts.T,
     )
 
 

time: 218 us -> 195 us (0.89)
  the two profiles are of different devices: /device:TPU:16 before, /device:TPU:84 now
where the time goes in v2:
time: 195 us
  Pallas kernels  193 us (99%)
  local copies, waits for them, and re-layouts  2 us (1%)
    pallas_call x1, Pallas kernels, per_device(): pl.pallas_call(functools.partial(kernel, nz, nx, gs), out_shape=(tile, ti...  193 us

profile of v2, /device:TPU:84, one launch (start us, length us, event | category | flops | bytes accessed | tf_op | source)
XLA Modules:
  0.0 195.2 jit_solution(10815612729312665909)
XLA Ops:
  0.6 192.6 %shard_map.158 = (bf16[128,128]{1,0:T(8,128)(2,1)}, bf16[128,128]{1,0:T(8,128)(2,1)}) custom-call(bf16[128,256]{1,0:T(8,128)(2,1)} %x_in.1, bf16[128,256]{1,0:T(8,128)(2,1)} %zg_in.1, bf16[128,128]{1,0:T(8,128)(2,1)} %b_in.1, bf16[128,128]{1,0:T(8,128)(2,1)} %c_in.1, f32[4,128]{1,0:T(4,128)} %dt_in.1, f32[4]{0:T(128)} %al_ref.1, f32[4]{0:T(128)} %dk_ref.1, ...), custom_call_target="tpu_custom_call" | custom-call | tf_op jit(solution)/shard_map/pallas_call | solution.py:750
  193.2 0.0 copy-start
  193.2 1.4 copy.19
  194.6 0.0 copy-done
  194.6 0.6 copy.20
Async XLA Ops:
  193.2 1.4 copy-start

commit v3 on v2

--- a/solution.py
+++ b/solution.py
@@ -57,8 +57,7 @@
     wu_in,
     wd_in,
     be_ref,
-    so_ref,
-    eo_ref,
+    out_ref,
     x_ref,
     zg_ref,
     b_ref,
@@ -97,7 +96,6 @@
     frcv,
     osnd,
     orcv,
-    flast,
     in_sem,
     wl_sem,
     ws_sem,
@@ -207,8 +205,16 @@
     def _():
         greet(opposite)
 
+    keeper = (2 * share + c, z)
+    summer = (2 * q + c, lax.rem(z + q, nx))
+
+    @pl.when(jnp.logical_and(q != z, z != 0))
+    def _():
+        greet(summer)
+
     peers = (
         (gs + ng + nx - 2)
+        + jnp.logical_and(share != z, q != z).astype(jnp.int32)
         + (member == gs - 1).astype(jnp.int32)
         + (member == 0).astype(jnp.int32)
         + apart.astype(jnp.int32)
@@ -438,6 +444,74 @@
     def _():
         to_opposite.start()
 
+    @pl.when(share != z)
+    def _():
+        to_opposite.wait_recv()
+        xs[share] = urcv[...]
+
+    @pl.when(share == z)
+    def _():
+        xs[share] = usnd[...]
+
+    def send_rows(o):
+        to = lax.rem(q + o, nx)
+        return remote(xs.at[share], xs.at[share], gs_sem.at[o], gr_sem.at[o], (ctx, to))
+
+    def rows_step(o, carry):
+        send_rows(o).start()
+        return carry
+
+    early = lax.rem(share - z + nz - hops_up + 1 + nz, nz) < 3
+
+    @pl.when(early)
+    def _():
+        lax.fori_loop(1, nx, rows_step, 0)
+
+    def rows_ready(d):
+        source = lax.rem(d + z, nx)
+        o = lax.rem(q - source + nx, nx)
+
+        @pl.when(o != 0)
+        def _():
+            remote(xs.at[d], xs.at[d], gs_sem.at[o], gr_sem.at[o], (ctx, source)).wait_recv()
+
+    for copy in w_sent:
+        copy.wait_recv()
+
+    def partial(d, k):
+        return mm(xs[d], wgu[be_ref[k, 2 * d + c]])
+
+    hops = (hops_up, hops_down)
+
+    def goes_up(way, k):
+        return (way == 0) == (k == 0)
+
+    def target(way, s, k):
+        if goes_up(way, k):
+            return lax.rem(z + hops[way] - s + nz, nz)
+        return lax.rem(z + nz - hops[way] + s, nz)
+
+    def send_sum(way, s, k):
+        return remote(
+            rp.at[way, s, k],
+            rp.at[way, s + 1, k],
+            rs_sem.at[way, s, k],
+            rr_sem.at[way, s, k],
+            (up if goes_up(way, k) else down, q),
+        )
+
+    rows_ready(lax.rem(z + hops_up, nz))
+    for far in (1, nz - 1):
+        rows_ready(lax.rem(z + hops_up + far, nz))
+    for k in range(2):
+        for way in range(2):
+            rp[way, 0, k] = partial(target(way, 0, k), k).astype(BF16)
+            send_sum(way, 0, k).start()
+
+    @pl.when(jnp.logical_not(early))
+    def _():
+        lax.fori_loop(1, nx, rows_step, 0)
+
     osnd[...] = stream.astype(BF16)
     stream_home = remote(osnd, orcv, ps_sem.at[0], pr_sem.at[0], home)
 
@@ -464,66 +538,6 @@
         return carry
 
     lax.fori_loop(1, nx, stat_step, 0)
-
-    @pl.when(share != z)
-    def _():
-        to_opposite.wait_recv()
-        xs[share] = urcv[...]
-
-    @pl.when(share == z)
-    def _():
-        xs[share] = usnd[...]
-
-    def send_rows(o):
-        to = lax.rem(q + o, nx)
-        return remote(xs.at[share], xs.at[share], gs_sem.at[o], gr_sem.at[o], (ctx, to))
-
-    def rows_step(o, carry):
-        send_rows(o).start()
-        return carry
-
-    lax.fori_loop(1, nx, rows_step, 0)
-
-    def rows_ready(d):
-        source = lax.rem(d + z, nx)
-        o = lax.rem(q - source + nx, nx)
-
-        @pl.when(o != 0)
-        def _():
-            remote(xs.at[d], xs.at[d], gs_sem.at[o], gr_sem.at[o], (ctx, source)).wait_recv()
-
-    for copy in w_sent:
-        copy.wait_recv()
-
-    def partial(d, k):
-        return mm(xs[d], wgu[be_ref[k, 2 * d + c]])
-
-    hops = (hops_up, hops_down)
-
-    def goes_up(way, k):
-        return (way == 0) == (k == 0)
-
-    def target(way, s, k):
-        if goes_up(way, k):
-            return lax.rem(z + hops[way] - s + nz, nz)
-        return lax.rem(z + nz - hops[way] + s, nz)
-
-    def send_sum(way, s, k):
-        return remote(
-            rp.at[way, s, k],
-            rp.at[way, s + 1, k],
-            rs_sem.at[way, s, k],
-            rr_sem.at[way, s, k],
-            (up if goes_up(way, k) else down, q),
-        )
-
-    rows_ready(lax.rem(z + hops_up, nz))
-    for far in (1, nz - 1):
-        rows_ready(lax.rem(z + hops_up + far, nz))
-    for k in range(2):
-        for way in range(2):
-            rp[way, 0, k] = partial(target(way, 0, k), k).astype(BF16)
-            send_sum(way, 0, k).start()
 
     def sum_hop(way, s, k):
         value = partial(target(way, s, k), k)
@@ -649,30 +663,30 @@
         return acc + ob[source].astype(F32)
 
     fsnd[...] = lax.fori_loop(1, nx, out_sum, os_[share].astype(F32)).astype(BF16)
-    to_owner = remote(fsnd, frcv, us_sem.at[1], ur_sem.at[1], opposite)
-    owner_home = remote(frcv, flast, ps_sem.at[1], pr_sem.at[1], home)
-
-    @pl.when(share != z)
-    def _():
-        to_owner.start()
-        to_owner.wait_recv()
-
-    @pl.when(share == z)
-    def _():
-        frcv[...] = fsnd[...]
+    to_keeper = remote(fsnd, frcv, us_sem.at[1], ur_sem.at[1], keeper)
+    moved = jnp.logical_or(share != z, q != z)
+
+    @pl.when(moved)
+    def _():
+        to_keeper.start()
 
     @pl.when(share != q)
     def _():
-        owner_home.start()
         stream_home.wait_recv()
-        so_ref[...] = orcv[...]
-        owner_home.wait_recv()
-        eo_ref[...] = flast[...]
+        out_ref[0] = orcv[...].astype(F32)
 
     @pl.when(share == q)
     def _():
-        so_ref[...] = osnd[...]
-        eo_ref[...] = frcv[...]
+        out_ref[0] = osnd[...].astype(F32)
+
+    @pl.when(moved)
+    def _():
+        to_keeper.wait_recv()
+        out_ref[1] = frcv[...].astype(F32)
+
+    @pl.when(jnp.logical_not(moved))
+    def _():
+        out_ref[1] = fsnd[...].astype(F32)
 
     for copy in (*w_sent, to_core, back):
         copy.wait_send()
@@ -687,12 +701,14 @@
     @pl.when(share != z)
     def _():
         to_opposite.wait_send()
-        to_owner.wait_send()
 
     @pl.when(share != q)
     def _():
         stream_home.wait_send()
-        owner_home.wait_send()
+
+    @pl.when(moved)
+    def _():
+        to_keeper.wait_send()
 
     def drain(o, carry):
         send_term(o).wait_send()
@@ -746,10 +762,9 @@
     hbm = pl.BlockSpec(memory_space=pl.ANY)
     dma = pltpu.SemaphoreType.DMA
     hops = nz // 2
-    tile = jax.ShapeDtypeStruct((T, T), BF16)
-    return pl.pallas_call(
+    both = pl.pallas_call(
         functools.partial(kernel, nz, nx, gs),
-        out_shape=(tile, tile),
+        out_shape=jax.ShapeDtypeStruct((2, T, T), F32),
         in_specs=[
             hbm,
             hbm,
@@ -767,7 +782,7 @@
             hbm,
             smem,
         ],
-        out_specs=(vmem, vmem),
+        out_specs=vmem,
         scratch_shapes=[
             pltpu.VMEM(x_in.shape, BF16),
             pltpu.VMEM(x_in.shape, BF16),
@@ -803,7 +818,6 @@
             pltpu.VMEM((nz, T, 512), BF16),
             pltpu.VMEM((nx, T, T), BF16),
             pltpu.VMEM((nx, T, T), BF16),
-            pltpu.VMEM((T, T), BF16),
             pltpu.VMEM((T, T), BF16),
             pltpu.VMEM((T, T), BF16),
             pltpu.VMEM((T, T), BF16),
@@ -855,6 +869,7 @@
         w_down,
         block_experts.T,
     )
+    return both[0].astype(BF16), both[1].astype(BF16)
 
 
 def solution(mesh):

time: 195 us -> 194 us (level)
  the two profiles are of different devices: /device:TPU:84 before, /device:TPU:16 now
where the time goes in v3:
time: 194 us; the launch traced here: 193 us
  Pallas kernels  191 us (98%)
    pallas_call x1, Pallas kernels, per_device(): pl.pallas_call(functools.partial(kernel, nz, nx, gs), out_shape=jax.Shape...  191 us

profile of v3, /device:TPU:16, one launch (start us, length us, event | category | flops | bytes accessed | tf_op | source)
XLA Modules:
  0.0 193.4 jit_solution(6306687531862362432)
XLA Ops:
  0.6 191.2 %shard_map.158 = f32[2,128,128]{2,1,0:T(8,128)} custom-call(bf16[128,256]{1,0:T(8,128)(2,1)} %x_in.1, bf16[128,256]{1,0:T(8,128)(2,1)} %zg_in.1, bf16[128,128]{1,0:T(8,128)(2,1)} %b_in.1, bf16[128,128]{1,0:T(8,128)(2,1)} %c_in.1, f32[4,128]{1,0:T(4,128)} %dt_in.1, f32[4]{0:T(128)} %al_ref.1, f32[4]{0:T(128)} %dk_ref.1, bf16[256,2048]{1,0:T(8,128)(2,1)} %op_in.1, ...), custom_call_target="tpu_custom_call" | custom-call | tf_op jit(solution)/shard_map/pallas_call | solution.py:765
  191.8 0.9 convert.4
  192.7 0.6 slice_bitcast_fusion

commit v4 on v3

--- a/solution.py
+++ b/solution.py
@@ -78,6 +78,8 @@
     gbuf,
     tmsg,
     tbuf,
+    entry,
+    shared,
     ysnd,
     yrcv,
     gt,
@@ -106,6 +108,8 @@
     ar_sem,
     bs_sem,
     br_sem,
+    es_sem,
+    er_sem,
     ts_sem,
     tr_sem,
     ss_sem,
@@ -355,8 +359,11 @@
         part = jnp.where(earlier, decay * part + s, part)
         part_a0 = jnp.where(earlier, part_a0 + a0, part_a0)
         part_a1 = jnp.where(earlier, part_a1 + a1, part_a1)
-    tmsg[0:T, :] = total.astype(BF16)
-    tmsg[T : T + 16, :] = log_rows(total_a0, total_a1)
+    some = T // gs
+    own_rows = pl.ds(pl.multiple_of(member * some, some), some)
+    entry[...] = total.astype(BF16)
+    tmsg[0:some, :] = entry[own_rows, :]
+    tmsg[some : some + 16, :] = log_rows(total_a0, total_a1)
 
     def to_group(o):
         to = 2 * (lax.rem(group + o, ng) * gs + member) + c
@@ -368,7 +375,7 @@
         def _(o=o):
             to_group(o).start()
 
-    reach = zero
+    reach = jnp.zeros((some, T), F32)
     for o in range(ng - 1, 0, -1):
 
         @pl.when(group >= o)
@@ -377,10 +384,23 @@
 
         @pl.when(group < o)
         def _(o=o):
-            tbuf[o] = jnp.zeros((T + 16, T), BF16)
-
-        s, a0, a1 = unpack(tbuf.at[o])
-        reach = jnp.where(group >= o, spread(a0, a1) * reach + s, zero)
+            tbuf[o] = jnp.zeros((some + 16, T), BF16)
+
+        tail = tbuf[o, some : some + 16, :].astype(F32)
+        log_total = jnp.where(member < gs // 2, tail[0:1] + tail[1:2], tail[2:3] + tail[3:4])
+        reach = jnp.exp(log_total) * reach + tbuf[o, 0:some, :].astype(F32)
+    shared[own_rows, :] = reach.astype(BF16)
+
+    def share_rows(o):
+        to = 2 * (group * gs + lax.rem(member + o, gs)) + c
+        rows = shared.at[own_rows, :]
+        return remote(rows, rows, es_sem.at[o], er_sem.at[o], (to, q))
+
+    for o in range(1, gs):
+        share_rows(o).start()
+    for o in range(1, gs):
+        share_rows(o).wait_recv()
+    reach = shared[...].astype(F32)
     at_first = spread(part_a0, part_a1) * reach + part
     at_second = spread(first_a0, first_a1) * at_first + first
     ysnd[...] = jnp.where(c == 0, at_second, at_first).astype(BF16)
@@ -692,6 +712,7 @@
         copy.wait_send()
     for o in range(1, gs):
         to_member(o).wait_send()
+        share_rows(o).wait_send()
     for o in range(1, ng):
 
         @pl.when(group + o < ng)
@@ -802,8 +823,10 @@
             pltpu.VMEM((T + 16, T), BF16),
             pltpu.VMEM((T + 16, T), BF16),
             pltpu.VMEM((gs, T + 16, T), BF16),
-            pltpu.VMEM((T + 16, T), BF16),
-            pltpu.VMEM((nz // gs, T + 16, T), BF16),
+            pltpu.VMEM((T // gs + 16, T), BF16),
+            pltpu.VMEM((nz // gs, T // gs + 16, T), BF16),
+            pltpu.VMEM((T, T), BF16),
+            pltpu.VMEM((T, T), BF16),
             pltpu.VMEM((T, T), BF16),
             pltpu.VMEM((T, T), BF16),
             pltpu.VMEM((nx, T, T), BF16),
@@ -832,6 +855,8 @@
             dma((gs,)),
             dma((nz // gs,)),
             dma((nz // gs,)),
+            dma((gs,)),
+            dma((gs,)),
             dma((nx,)),
             dma((nx,)),
             dma((nx,)),

time: 194 us -> 194 us (level)
  no operation moved by 1% of the time
where the time goes in v4:
time: 194 us
  Pallas kernels  191 us (98%)
    pallas_call x1, Pallas kernels, per_device(): pl.pallas_call(functools.partial(kernel, nz, nx, gs), out_shape=jax.Shape...  191 us

profile of v4, /device:TPU:16, one launch (start us, length us, event | category | flops | bytes accessed | tf_op | source)
XLA Modules:
  0.0 193.5 jit_solution(4770268684318304694)
XLA Ops:
  0.6 191.3 %shard_map.158 = f32[2,128,128]{2,1,0:T(8,128)} custom-call(bf16[128,256]{1,0:T(8,128)(2,1)} %x_in.1, bf16[128,256]{1,0:T(8,128)(2,1)} %zg_in.1, bf16[128,128]{1,0:T(8,128)(2,1)} %b_in.1, bf16[128,128]{1,0:T(8,128)(2,1)} %c_in.1, f32[4,128]{1,0:T(4,128)} %dt_in.1, f32[4]{0:T(128)} %al_ref.1, f32[4]{0:T(128)} %dk_ref.1, bf16[256,2048]{1,0:T(8,128)(2,1)} %op_in.1, ...), custom_call_target="tpu_custom_call" | custom-call | tf_op jit(solution)/shard_map/pallas_call | solution.py:786
  192.0 0.9 convert.4
  192.9 0.6 slice_bitcast_fusion
